TPU v7x, 128 devices: a whole 4x4x4 slice. The times are simulated.
128 devices in a mesh: bulk: 8 (over x, core), wide: 16 (over y, z).
Axes of the slice: x: 4, y: 4, z: 4, core: 2. Of those that a mesh axis runs over, the one named last changes fastest.
Arguments:
- held: float32 [4096, 128, 256], P(('bulk', 'wide')), as said below
- source_slot: int32 [2048], P(('bulk', 'wide')), may hold values from 0 to 31, as said below
Outputs:
- q_factor: float32 [262144, 256], P(('bulk', 'wide'))
- r_factor: float32 [256, 256], replicated
Inputs may be any that keep to these rules, and one draw needn't show every extreme that they name: `source_slot`: for each slab the 16 entries are distinct; one value of c = entry // 4 is used by 4 blocks, six others by two blocks each (entries c * 4 and c * 4 + 1). Slots of held that no entry of source_slot names are zero.
All inputs are finite; a program needn't handle non-finite values.
Results may differ from a plain program's by a relative error of at most 0.000073.
Values sent between devices are 32-bit elements; how exact they have to be, the bound alone decides.
A program may use at most 64 MiB of HBM per device.

v0:
```python
import jax
import jax.numpy as jnp
from jax import lax
from jax.sharding import PartitionSpec as P

CP = 4
W = 8


def from_behind(value, axis, steps):
    count = lax.axis_size(axis)
    pairs = [(source, (source + steps) % count) for source in range(count)]
    return lax.ppermute(value, axis, pairs)


def swapped(block, axis, apart):
    count = lax.axis_size(axis)
    route = []
    for low in range(count):
        high = low | 1 << apart
        if high != low and high < count:
            route += [(low, high), (high, low)]
    return lax.ppermute(block, axis, route)


def regrid(buffer, source_slot):
    pieces = [buffer[0:CP]]
    for offset in range(1, W):
        moved = from_behind(buffer[offset * CP : (offset + 1) * CP], ("bulk", "wide"), -offset)
        pieces.append(moved)
    received = jnp.concatenate(pieces, axis=0)
    chosen = jnp.take(received, source_slot, axis=0)
    return chosen.reshape(-1, buffer.shape[2])


def gram_of(matrix, total):
    product = lax.dot_general(
        matrix,
        matrix,
        (((0,), (0,)), ((), ())),
        precision=lax.Precision.HIGHEST,
        preferred_element_type=jnp.float32,
    )
    return product / total


def merged(gram):
    for bit in range(lax.axis_size("bulk").bit_length() - 1):
        gram = gram + swapped(gram, "bulk", bit)
    for bit in range(lax.axis_size("wide").bit_length() - 1):
        gram = gram + swapped(gram, "wide", bit)
    return gram


def factor(gram):
    lower = jnp.linalg.cholesky(gram)
    identity = jnp.eye(gram.shape[0], dtype=jnp.float32)
    inverse = jax.scipy.linalg.solve_triangular(lower, identity, lower=True)
    return (lower.T, inverse)


def solved(inverse, matrix):
    return lax.dot_general(
        matrix,
        inverse,
        (((1,), (1,)), ((), ())),
        precision=lax.Precision.HIGHEST,
        preferred_element_type=jnp.float32,
    )


def local(held, source_slot):
    total = lax.axis_size("bulk") * lax.axis_size("wide") * source_slot.shape[0] * held.shape[1]
    slab_rows = regrid(held, source_slot)
    r_factor, inverse = factor(merged(gram_of(slab_rows, total)))
    q_factor = solved(inverse, slab_rows)
    return (q_factor, r_factor)


def solution(mesh):
    in_specs = (P(("bulk", "wide"), None, None), P(("bulk", "wide")))
    out_specs = (P(("bulk", "wide"), None), P())
    return jax.shard_map(local, mesh=mesh, in_specs=in_specs, out_specs=out_specs, check_vma=False)
```

profile of v0, /device:TPU:24, one launch (start us, length us, event | category | flops | bytes accessed | tf_op | source)
XLA Modules:
  0.0 249.1 jit_solution(11668063618168330865)
XLA Ops:
  0.6 3.3 %fusion.27 = (f32[4,128,256]{2,1,0:T(8,128)S(1)}, f32[4,128,256]{2,1,0:T(8,128)S(1)}, f32[4,128,256]{2,1,0:T(8,128)S(1)}, f32[4,128,256]{2,1,0:T(8,128)S(1)}, f3...) fusion(f32[32,128,256]{2,1,0:T(8,128)} %param.2), kind=kLoop, calls=%fused_computation.57 | loop fusion | bytes 8388608 | tf_op jit(solution)/shard_map/slice | solution.py:29
  4.0 4.2 %collective-permute-start = (f32[4,128,256]{2,1,0:T(8,128)S(1)}, f32[4,128,256]{2,1,0:T(8,128)S(1)}, u32[]{:S(2)}, u32[]{:S(2)}) collective-permute-start(f32[4,128,256]{2,1,0:T(8,128)S(1)} %get-tuple-element.27), channel_id=1, source_target_pairs={{0,127},{1,0},{2,1},{3,2},{4,3},{5,4},{6,5},{7,6},{8,7},{9,8},{10,... | collective-permute-start | bytes 1572872 | tf_op jit(solution)/shard_map/ppermute | solution.py:13
  9.8 6.7 %collective-permute-start.4 = (f32[4,128,256]{2,1,0:T(8,128)S(1)}, f32[4,128,256]{2,1,0:T(8,128)S(1)}, u32[]{:S(2)}, u32[]{:S(2)}) collective-permute-start(f32[4,128,256]{2,1,0:T(8,128)S(1)} %get-tuple-element.23), channel_id=1, source_target_pairs={{0,123},{1,124},{2,125},{3,126},{4,127},{5,0},{6,1},{7,2},{8,3},{9... | collective-permute-start | bytes 1572872 | tf_op jit(solution)/shard_map/ppermute | solution.py:13
  16.5 20.6 %collective-permute-done = f32[4,128,256]{2,1,0:T(8,128)S(1)} collective-permute-done((f32[4,128,256]{2,1,0:T(8,128)S(1)}, f32[4,128,256]{2,1,0:T(8,128)S(1)}, u32[]{:S(2)}, u32[]{:S(2)}) %collective-permute-start) | collective-permute-done | bytes 524320 | tf_op jit(solution)/shard_map/ppermute | solution.py:13
  37.9 16.3 %collective-permute-done.1 = f32[4,128,256]{2,1,0:T(8,128)S(1)} collective-permute-done((f32[4,128,256]{2,1,0:T(8,128)S(1)}, f32[4,128,256]{2,1,0:T(8,128)S(1)}, u32[]{:S(2)}, u32[]{:S(2)}) %collective-permute-start.1) | collective-permute-done | bytes 524320 | tf_op jit(solution)/shard_map/ppermute | solution.py:13
  54.2 11.2 %collective-permute-start.6 = (f32[4,128,256]{2,1,0:T(8,128)S(1)}, f32[4,128,256]{2,1,0:T(8,128)S(1)}, u32[]{:S(2)}, u32[]{:S(2)}) collective-permute-start(f32[4,128,256]{2,1,0:T(8,128)S(1)} %get-tuple-element.22), channel_id=1, source_target_pairs={{0,121},{1,122},{2,123},{3,124},{4,125},{5,126},{6,127},{7,0},{8,1... | collective-permute-start | bytes 1572872 | tf_op jit(solution)/shard_map/ppermute | solution.py:13
  66.2 9.6 %collective-permute-done.2 = f32[4,128,256]{2,1,0:T(8,128)S(1)} collective-permute-done((f32[4,128,256]{2,1,0:T(8,128)S(1)}, f32[4,128,256]{2,1,0:T(8,128)S(1)}, u32[]{:S(2)}, u32[]{:S(2)}) %collective-permute-start.2) | collective-permute-done | bytes 524320 | tf_op jit(solution)/shard_map/ppermute | solution.py:13
  76.7 10.4 %collective-permute-done.3 = f32[4,128,256]{2,1,0:T(8,128)S(1)} collective-permute-done((f32[4,128,256]{2,1,0:T(8,128)S(1)}, f32[4,128,256]{2,1,0:T(8,128)S(1)}, u32[]{:S(2)}, u32[]{:S(2)}) %collective-permute-start.3) | collective-permute-done | bytes 524320 | tf_op jit(solution)/shard_map/ppermute | solution.py:13
  88.0 10.4 %collective-permute-done.4 = f32[4,128,256]{2,1,0:T(8,128)S(1)} collective-permute-done((f32[4,128,256]{2,1,0:T(8,128)S(1)}, f32[4,128,256]{2,1,0:T(8,128)S(1)}, u32[]{:S(2)}, u32[]{:S(2)}) %collective-permute-start.4) | collective-permute-done | bytes 524320 | tf_op jit(solution)/shard_map/ppermute | solution.py:13
  99.2 10.4 %collective-permute-done.5 = f32[4,128,256]{2,1,0:T(8,128)S(1)} collective-permute-done((f32[4,128,256]{2,1,0:T(8,128)S(1)}, f32[4,128,256]{2,1,0:T(8,128)S(1)}, u32[]{:S(2)}, u32[]{:S(2)}) %collective-permute-start.5) | collective-permute-done | bytes 524320 | tf_op jit(solution)/shard_map/ppermute | solution.py:13
  110.4 9.2 %collective-permute-done.6 = f32[4,128,256]{2,1,0:T(8,128)S(1)} collective-permute-done((f32[4,128,256]{2,1,0:T(8,128)S(1)}, f32[4,128,256]{2,1,0:T(8,128)S(1)}, u32[]{:S(2)}, u32[]{:S(2)}) %collective-permute-start.6) | collective-permute-done | bytes 524320 | tf_op jit(solution)/shard_map/ppermute | solution.py:13
  123.4 3.6 %fusion.5 = f32[256,256]{0,1:T(8,128)S(1)} fusion(f32[16,128,256]{2,1,0:T(8,128)S(1)} %gather_fusion, pred[16]{0:T(512)(128)(4,1)S(1)} %compare_and_fusion), kind=kOutput, calls=%fused_computation.7 | convolution fusion | flops 1611202560 | bytes 2359312 | tf_op jit(solution)/shard_map/dot_general | solution.py:37
  130.2 6.9 %collective-permute-done.8 = f32[256,256]{0,1:T(8,128)S(1)} collective-permute-done((f32[256,256]{0,1:T(8,128)S(1)}, f32[256,256]{0,1:T(8,128)S(1)}, u32[]{:S(2)}, u32[]{:S(2)}) %collective-permute-start.8) | collective-permute-done | bytes 262176 | tf_op jit(solution)/shard_map/ppermute | solution.py:23
  139.9 6.3 %collective-permute-done.9 = f32[256,256]{0,1:T(8,128)S(1)} collective-permute-done((f32[256,256]{0,1:T(8,128)S(1)}, f32[256,256]{0,1:T(8,128)S(1)}, u32[]{:S(2)}, u32[]{:S(2)}) %collective-permute-start.9) | collective-permute-done | bytes 262176 | tf_op jit(solution)/shard_map/ppermute | solution.py:23
  146.2 7.7 %collective-permute-start.10 = (f32[256,256]{0,1:T(8,128)S(1)}, f32[256,256]{0,1:T(8,128)S(1)}, u32[]{:S(2)}, u32[]{:S(2)}) collective-permute-start(f32[256,256]{0,1:T(8,128)S(1)} %add.51), channel_id=1, source_target_pairs={{0,1},{1,0},{2,3},{3,2},{4,5},{5,4},{6,7},{7,6},{8,9},{9,8},{10,11... | collective-permute-start | bytes 786440 | tf_op jit(solution)/shard_map/ppermute | solution.py:23
  153.9 5.2 %collective-permute-done.10 = f32[256,256]{0,1:T(8,128)S(1)} collective-permute-done((f32[256,256]{0,1:T(8,128)S(1)}, f32[256,256]{0,1:T(8,128)S(1)}, u32[]{:S(2)}, u32[]{:S(2)}) %collective-permute-start.10) | collective-permute-done | bytes 262176 | tf_op jit(solution)/shard_map/ppermute | solution.py:23
  159.3 7.8 %collective-permute-done.11 = f32[256,256]{0,1:T(8,128)S(1)} collective-permute-done((f32[256,256]{0,1:T(8,128)S(1)}, f32[256,256]{0,1:T(8,128)S(1)}, u32[]{:S(2)}, u32[]{:S(2)}) %collective-permute-start.11) | collective-permute-done | bytes 262176 | tf_op jit(solution)/shard_map/ppermute | solution.py:23
  167.3 9.0 %collective-permute-done.12 = f32[256,256]{0,1:T(8,128)S(1)} collective-permute-done((f32[256,256]{0,1:T(8,128)S(1)}, f32[256,256]{0,1:T(8,128)S(1)}, u32[]{:S(2)}, u32[]{:S(2)}) %collective-permute-start.12) | collective-permute-done | bytes 262176 | tf_op jit(solution)/shard_map/ppermute | solution.py:23
  178.3 6.2 %collective-permute-done.13 = f32[256,256]{0,1:T(8,128)S(1)} collective-permute-done((f32[256,256]{0,1:T(8,128)S(1)}, f32[256,256]{0,1:T(8,128)S(1)}, u32[]{:S(2)}, u32[]{:S(2)}) %collective-permute-start.13) | collective-permute-done | bytes 262176 | tf_op jit(solution)/shard_map/ppermute | solution.py:23
  184.8 11.7 %cholesky.50 = f32[128,128]{1,0:T(8,128)S(1)} custom-call(f32[128,128]{1,0:T(8,128)S(1)} %cholesky.118), custom_call_target="Cholesky" | custom-call | tf_op jit(solution)/shard_map/jit(cholesky)/cholesky | solution.py:56
  196.5 9.8 %custom-call.15 = f32[1,128,128]{1,2,0:T(8,128)S(1)} custom-call(f32[1,128,128]{2,1,0:T(8,128)S(1)} %get-tuple-element.35), custom_call_target="InvertDiagBlocksLowerTriangular" | custom-call | tf_op jit(solution)/shard_map/jit(cholesky)/cholesky | solution.py:56
  206.8 11.7 %cholesky.105 = f32[128,128]{1,0:T(8,128)S(1)} custom-call(f32[128,128]{1,0:T(8,128)S(1)} %slice_subtract_fusion), custom_call_target="Cholesky" | custom-call | tf_op jit(solution)/shard_map/jit(cholesky)/cholesky | solution.py:56
  220.6 4.0 %while.1 = (s32[]{:T(128)}, f32[256,256]{1,0:T(8,128)S(1)}, s32[2,2]{1,0:T(2,128)S(1)}, f32[2,128,128]{2,1,0:T(8,128)S(1)}, s32[]{:T(128)}) while((s32[]{:T(128)}, f32[256,256]{1,0:T(8,128)S(1)}, s32[2,2]{1,0:T(2,128)S(1)}, f32[2,128,128]{2,1,0:T(8,128)S(1)}, s32[]{:T(128)}) %tuple.36), condition=%wide.while_cond, body=%wide.while_body.sunk | while | flops 2 | bytes 131181 | solution.py:58
  224.6 19.7 %custom-call.16 = f32[2,128,128]{1,2,0:T(8,128)S(1)} custom-call(f32[2,128,128]{2,1,0:T(8,128)S(1)} %get-tuple-element.9), custom_call_target="InvertDiagBlocksLowerTriangular" | custom-call | tf_op jit(solution)/shard_map/jit(_solve_triangular)/triangular_solve | solution.py:58
  (60 shorter events, 29.0 us)
Async XLA Ops:
  0.6 15.8 %copy-start.1 = (s32[16]{0:T(128)S(1)}, s32[16]{0:T(128)}, u32[]{:S(2)}) copy-start(s32[16]{0:T(128)} %param.3) | copy-start | bytes 196
  4.0 33.1 %collective-permute-start = (f32[4,128,256]{2,1,0:T(8,128)S(1)}, f32[4,128,256]{2,1,0:T(8,128)S(1)}, u32[]{:S(2)}, u32[]{:S(2)}) collective-permute-start(f32[4,128,256]{2,1,0:T(8,128)S(1)} %get-tuple-element.27), channel_id=1, source_target_pairs={{0,127},{1,0},{2,1},{3,2},{4,3},{5,4},{6,5},{7,6},{8,7},{9,8},{10,... | collective-permute-start | bytes 1572872 | tf_op jit(solution)/shard_map/ppermute | solution.py:13
  8.2 46.0 %collective-permute-start.1 = (f32[4,128,256]{2,1,0:T(8,128)S(1)}, f32[4,128,256]{2,1,0:T(8,128)S(1)}, u32[]{:S(2)}, u32[]{:S(2)}) collective-permute-start(f32[4,128,256]{2,1,0:T(8,128)S(1)} %get-tuple-element.26), channel_id=1, source_target_pairs={{0,126},{1,127},{2,0},{3,1},{4,2},{5,3},{6,4},{7,5},{8,6},{9,7},{1... | collective-permute-start | bytes 1572872 | tf_op jit(solution)/shard_map/ppermute | solution.py:13
  8.2 67.7 %collective-permute-start.2 = (f32[4,128,256]{2,1,0:T(8,128)S(1)}, f32[4,128,256]{2,1,0:T(8,128)S(1)}, u32[]{:S(2)}, u32[]{:S(2)}) collective-permute-start(f32[4,128,256]{2,1,0:T(8,128)S(1)} %get-tuple-element.25), channel_id=1, source_target_pairs={{0,125},{1,126},{2,127},{3,0},{4,1},{5,2},{6,3},{7,4},{8,5},{9,6},... | collective-permute-start | bytes 1572872 | tf_op jit(solution)/shard_map/ppermute | solution.py:13
  9.3 77.8 %collective-permute-start.3 = (f32[4,128,256]{2,1,0:T(8,128)S(1)}, f32[4,128,256]{2,1,0:T(8,128)S(1)}, u32[]{:S(2)}, u32[]{:S(2)}) collective-permute-start(f32[4,128,256]{2,1,0:T(8,128)S(1)} %get-tuple-element.24), channel_id=1, source_target_pairs={{0,124},{1,125},{2,126},{3,127},{4,0},{5,1},{6,2},{7,3},{8,4},{9,5... | collective-permute-start | bytes 1572872 | tf_op jit(solution)/shard_map/ppermute | solution.py:13
  9.8 88.5 %collective-permute-start.4 = (f32[4,128,256]{2,1,0:T(8,128)S(1)}, f32[4,128,256]{2,1,0:T(8,128)S(1)}, u32[]{:S(2)}, u32[]{:S(2)}) collective-permute-start(f32[4,128,256]{2,1,0:T(8,128)S(1)} %get-tuple-element.23), channel_id=1, source_target_pairs={{0,123},{1,124},{2,125},{3,126},{4,127},{5,0},{6,1},{7,2},{8,3},{9... | collective-permute-start | bytes 1572872 | tf_op jit(solution)/shard_map/ppermute | solution.py:13
  37.1 72.5 %collective-permute-start.5 = (f32[4,128,256]{2,1,0:T(8,128)S(1)}, f32[4,128,256]{2,1,0:T(8,128)S(1)}, u32[]{:S(2)}, u32[]{:S(2)}) collective-permute-start(f32[4,128,256]{2,1,0:T(8,128)S(1)} %get-tuple-element.29), channel_id=1, source_target_pairs={{0,122},{1,123},{2,124},{3,125},{4,126},{5,127},{6,0},{7,1},{8,2},... | collective-permute-start | bytes 1572872 | tf_op jit(solution)/shard_map/ppermute | solution.py:13
  54.2 65.5 %collective-permute-start.6 = (f32[4,128,256]{2,1,0:T(8,128)S(1)}, f32[4,128,256]{2,1,0:T(8,128)S(1)}, u32[]{:S(2)}, u32[]{:S(2)}) collective-permute-start(f32[4,128,256]{2,1,0:T(8,128)S(1)} %get-tuple-element.22), channel_id=1, source_target_pairs={{0,121},{1,122},{2,123},{3,124},{4,125},{5,126},{6,127},{7,0},{8,1... | collective-permute-start | bytes 1572872 | tf_op jit(solution)/shard_map/ppermute | solution.py:13
  127.0 1.6 collective-permute-start.7
  128.6 8.4 %collective-permute-start.8 = (f32[256,256]{0,1:T(8,128)S(1)}, f32[256,256]{0,1:T(8,128)S(1)}, u32[]{:S(2)}, u32[]{:S(2)}) collective-permute-start(f32[256,256]{0,1:T(8,128)S(1)} %add.49), channel_id=1, source_target_pairs={{0,32},{32,0},{16,48},{48,16},{64,96},{96,64},{80,112},{112,80},{1... | collective-permute-start | bytes 786440 | tf_op jit(solution)/shard_map/ppermute | solution.py:23
  137.1 9.1 %collective-permute-start.9 = (f32[256,256]{0,1:T(8,128)S(1)}, f32[256,256]{0,1:T(8,128)S(1)}, u32[]{:S(2)}, u32[]{:S(2)}) collective-permute-start(f32[256,256]{0,1:T(8,128)S(1)} %add.50), channel_id=1, source_target_pairs={{0,64},{64,0},{16,80},{80,16},{32,96},{96,32},{48,112},{112,48},{1... | collective-permute-start | bytes 786440 | tf_op jit(solution)/shard_map/ppermute | solution.py:23
  146.2 12.9 %collective-permute-start.10 = (f32[256,256]{0,1:T(8,128)S(1)}, f32[256,256]{0,1:T(8,128)S(1)}, u32[]{:S(2)}, u32[]{:S(2)}) collective-permute-start(f32[256,256]{0,1:T(8,128)S(1)} %add.51), channel_id=1, source_target_pairs={{0,1},{1,0},{2,3},{3,2},{4,5},{5,4},{6,7},{7,6},{8,9},{9,8},{10,11... | collective-permute-start | bytes 786440 | tf_op jit(solution)/shard_map/ppermute | solution.py:23
  159.1 8.0 %collective-permute-start.11 = (f32[256,256]{0,1:T(8,128)S(1)}, f32[256,256]{0,1:T(8,128)S(1)}, u32[]{:S(2)}, u32[]{:S(2)}) collective-permute-start(f32[256,256]{0,1:T(8,128)S(1)} %add.52), channel_id=1, source_target_pairs={{0,2},{2,0},{1,3},{3,1},{4,6},{6,4},{5,7},{7,5},{8,10},{10,8},{9,1... | collective-permute-start | bytes 786440 | tf_op jit(solution)/shard_map/ppermute | solution.py:23
  167.1 9.2 %collective-permute-start.12 = (f32[256,256]{0,1:T(8,128)S(1)}, f32[256,256]{0,1:T(8,128)S(1)}, u32[]{:S(2)}, u32[]{:S(2)}) collective-permute-start(f32[256,256]{0,1:T(8,128)S(1)} %add.53), channel_id=1, source_target_pairs={{0,4},{4,0},{1,5},{5,1},{2,6},{6,2},{3,7},{7,3},{8,12},{12,8},{9,1... | collective-permute-start | bytes 786440 | tf_op jit(solution)/shard_map/ppermute | solution.py:23
  176.4 8.1 %collective-permute-start.13 = (f32[256,256]{0,1:T(8,128)S(1)}, f32[256,256]{0,1:T(8,128)S(1)}, u32[]{:S(2)}, u32[]{:S(2)}) collective-permute-start(f32[256,256]{0,1:T(8,128)S(1)} %add.54), channel_id=1, source_target_pairs={{0,8},{8,0},{1,9},{9,1},{2,10},{10,2},{3,11},{11,3},{4,12},{12,4},... | collective-permute-start | bytes 786440 | tf_op jit(solution)/shard_map/ppermute | solution.py:23
  178.3 67.6 %copy-start = (f32[2048,256]{1,0:T(8,128)S(1)}, f32[2048,256]{1,0:T(8,128)}, u32[]{:S(2)}) copy-start(f32[2048,256]{1,0:T(8,128)} %bitcast_select_fusion) | copy-start | bytes 6291460
where the time goes:
time: 249 us
  waiting for transfers between devices  130 us (52%)
  other arithmetic  55.7 us (22%)
  starting transfers between devices  36.3 us (15%)
  local copies, waits for them, and re-layouts  17.1 us (7%)
  matrix products  8.07 us (3%)
    ppermute x7, waiting for transfers between devices, from_behind(): return lax.ppermute(value, axis, pairs)  86.9 us
    ppermute x7, waiting for transfers between devices, swapped(): return lax.ppermute(block, axis, route)  42.9 us
    another operation x6, other arithmetic, factor(): lower = jnp.linalg.cholesky(gram)  34 us
    ppermute x7, starting transfers between devices, from_behind(): return lax.ppermute(value, axis, pairs)  23.7 us
    another operation x2, other arithmetic, factor(): inverse = jax.scipy.linalg.solve_triangular(lower, identity, lower=True)  19.7 us
    ppermute x7, starting transfers between devices, swapped(): return lax.ppermute(block, axis, route)  12.6 us
    unnamed x11, local copies, waits for them, and re-layouts  5.94 us
  transfers between devices with their start and end apart: 14, of which 14 were waited for; matrix products, arithmetic and copies ran while one was open for 3% of the time, Pallas kernels for 0%

commit v1 on v0

v1 whole, which is shorter than its diff:
```python
import functools

import jax
import jax.numpy as jnp
from jax import lax
from jax.experimental import pallas as pl
from jax.experimental.pallas import tpu as pltpu
from jax.sharding import PartitionSpec as P

CP = 4
W = 8
KEPT = 2
MESH = pl.DeviceIdType.MESH
TILE = 8
HALF = 128
F32 = jnp.float32
BF16 = jnp.bfloat16


def row_of(x, r):
    return jnp.broadcast_to(x[r : r + 1, :], x.shape)


def col_of(x, c):
    return jnp.broadcast_to(x[:, c : c + 1], x.shape)


def reciprocal(x):
    y = pl.reciprocal(x, approx=True)
    return y * (2.0 - x * y)


def panels(a):
    count = HALF // TILE
    a = list(a)
    sub = lax.broadcasted_iota(jnp.int32, (TILE, HALF), 0)
    lane = lax.broadcasted_iota(jnp.int32, (TILE, HALF), 1)
    e = [jnp.where(lane == sub + TILE * t, 1.0, 0.0) for t in range(count)]
    upper, inverse = [], []
    for p in range(count):
        at = TILE * p
        cols = [col_of(a[p], at + q) for q in range(TILE)]
        d = {(i, j): row_of(cols[j], i) for i in range(TILE) for j in range(i, TILE)}
        y, z, l, inv = [], [], {}, []
        for r in range(TILE):
            yr, zr = row_of(a[p], r), row_of(e[p], r)
            for q in range(r):
                yr = yr - l[r, q] * y[q]
                zr = zr - l[r, q] * z[q]
            y.append(yr)
            z.append(zr)
            inv.append(reciprocal(d[r, r]))
            for i in range(r + 1, TILE):
                l[i, r] = d[r, i] * inv[r]
            for i in range(r + 1, TILE):
                for j in range(i, TILE):
                    d[i, j] = d[i, j] - l[i, r] * d[r, j]
        scale = lax.rsqrt(d[0, 0])
        rows_y, rows_z = y[0] * scale, z[0] * scale
        for r in range(1, TILE):
            scale = lax.rsqrt(d[r, r])
            rows_y = jnp.where(sub == r, y[r] * scale, rows_y)
            rows_z = jnp.where(sub == r, z[r] * scale, rows_z)
        upper.append(jnp.where(lane >= sub + at, rows_y, 0.0))
        inverse.append(jnp.where(lane <= sub + at, rows_z, 0.0))
        y = [y[r] * inv[r] for r in range(TILE)]
        z = [z[r] * inv[r] for r in range(TILE)]
        if p + 1 < count:
            c = [col_of(a[p + 1], at + q) for q in range(TILE)]
            for r in range(TILE):
                for q in range(r):
                    c[r] = c[r] - l[r, q] * c[q]
            for r in range(TILE):
                a[p + 1] = a[p + 1] - c[r] * y[r]
                e[p + 1] = e[p + 1] - c[r] * z[r]
        if p + 2 < count:
            for r in reversed(range(TILE)):
                for q in range(r + 1, TILE):
                    y[r] = y[r] - l[q, r] * y[q]
                    z[r] = z[r] - l[q, r] * z[q]
            for t in range(p + 2, count):
                c = [col_of(a[t], at + q) for q in range(TILE)]
                for r in range(TILE):
                    a[t] = a[t] - c[r] * y[r]
                    e[t] = e[t] - c[r] * z[r]
    return upper, inverse


def dot(x, y, over):
    return lax.dot_general(
        x, y, (over, ((), ())), precision=lax.Precision.HIGHEST, preferred_element_type=F32
    )


def split(x):
    high = x.astype(BF16)
    return high, (x - high.astype(F32)).astype(BF16)


def half_dot(x, y, over):
    return lax.dot_general(x, y, (over, ((), ())), preferred_element_type=F32)


def factored(gram, r_ref, w_ref, work, cross, between):
    n = HALF
    work[...] = gram[0:n, 0:n]
    r_ref[n:, 0:n] = jnp.zeros((n, n), F32)
    w_ref[0:n, n:] = jnp.zeros((n, n), F32)

    def half(h, carry):
        up, inv = panels([work[TILE * t : TILE * (t + 1), :] for t in range(n // TILE)])

        @pl.when(h == 0)
        def _():
            for t in range(n // TILE):
                r_ref[TILE * t : TILE * (t + 1), 0:n] = up[t]
                w_ref[TILE * t : TILE * (t + 1), 0:n] = inv[t]
            w = w_ref[0:n, 0:n]
            right = dot(w, gram[0:n, n:], ((1,), (0,)))
            r_ref[0:n, n:] = right
            work[...] = gram[n:, n:] - dot(right, right, ((0,), (0,)))
            cross[...] = dot(right, w, ((0,), (0,)))
            between()

        @pl.when(h == 1)
        def _():
            for t in range(n // TILE):
                r_ref[n + TILE * t : n + TILE * (t + 1), n:] = up[t]
                w_ref[n + TILE * t : n + TILE * (t + 1), n:] = inv[t]
            w_ref[n:, 0:n] = -dot(w_ref[n:, n:], cross[...], ((1,), (0,)))

        return carry

    lax.fori_loop(0, 2, half, 0)


def window(
    bulk, wide, total,
    held, got, r_ref, w_ref,
    own, acc, parts, shares, gram, flat, work, cross, once, twice, thrice,
    load_sem, part_send, part_recv, share_send, share_recv, gram_send, gram_recv,
    slab_send, slab_recv, tree_send, tree_recv, keep_sem,
):
    my_bulk, my_wide = lax.axis_index("bulk"), lax.axis_index("wide")
    me = my_bulk * wide + my_wide
    devices = bulk * wide

    def along_wide(o):
        return (my_bulk, lax.rem(my_wide + o, wide))

    def along_bulk(o):
        return (lax.rem(my_bulk + o, bulk), my_wide)

    def behind(c):
        to = lax.rem(me + devices - c, devices)
        return (to // wide, lax.rem(to, wide))

    def remote(src, dst, send, recv, to):
        return pltpu.make_async_remote_copy(
            src_ref=src, dst_ref=dst, send_sem=send, recv_sem=recv, device_id=to, device_id_type=MESH
        )

    loads = [
        pltpu.make_async_copy(held.at[pl.ds(c * CP, CP)], own.at[pl.ds(c * CP, CP)], load_sem.at[c])
        for c in range(W)
    ]
    for load in loads:
        load.start()

    barrier = pltpu.get_barrier_semaphore()
    peers = [along_wide(o) for o in range(1, wide)] + [along_bulk(o) for o in range(1, bulk)]
    peers += [behind(c) for c in range(1, W)] + [behind(devices - c) for c in range(1, W)]
    for peer in peers:
        pl.semaphore_signal(barrier, inc=1, device_id=peer, device_id_type=MESH)
    pl.semaphore_wait(barrier, len(peers))

    first = [
        remote(
            held.at[pl.ds((2 * j + 1) * CP + KEPT, CP - KEPT)], once.at[j],
            tree_send.at[j], tree_recv.at[j], behind(1),
        )
        for j in range(W // 2)
    ]
    for copy in first:
        copy.start()
    straight = [
        remote(
            held.at[pl.ds(c * CP, KEPT)], got.at[pl.ds(c * KEPT, KEPT)],
            slab_send.at[c], slab_recv.at[c], behind(c),
        )
        for c in range(1, W)
    ]
    for copy in straight:
        copy.start()
    keep = pltpu.make_async_copy(held.at[pl.ds(0, KEPT)], got.at[pl.ds(0, KEPT)], keep_sem.at[0])
    keep.start()

    rows, k = CP * own.shape[1], own.shape[2]
    square, mixed = jnp.zeros((k, k), F32), jnp.zeros((k, k), F32)
    for c in range(W):
        loads[c].wait()
        high, low = split(own[c * CP : (c + 1) * CP].reshape(rows, k))
        square += half_dot(high, high, ((0,), (0,))) + half_dot(low, low, ((0,), (0,)))
        mixed += half_dot(high, low, ((0,), (0,)))
    acc[...] = (square + mixed + mixed.T).reshape(acc.shape)

    copies = [
        remote(acc.at[along_wide(o)[1]], parts.at[o], part_send.at[o], part_recv.at[o], along_wide(o))
        for o in range(1, wide)
    ]
    for copy in copies:
        copy.start()
    share = acc[my_wide]
    for o in range(1, wide):
        copies[o - 1].wait_recv()
        share += parts[o]
    shares[my_bulk] = share
    for copy in copies:
        copy.wait_send()
    copies = [
        remote(shares.at[my_bulk], shares.at[my_bulk], share_send.at[o], share_recv.at[o], along_bulk(o))
        for o in range(1, bulk)
    ]
    for copy in copies:
        copy.start()
    for copy in copies:
        copy.wait()
    share = shares[0]
    for b in range(1, bulk):
        share += shares[b]
    gram[my_wide] = share
    copies = [
        remote(gram.at[my_wide], gram.at[my_wide], gram_send.at[o], gram_recv.at[o], along_wide(o))
        for o in range(1, wide)
    ]
    for copy in copies:
        copy.start()
    for copy in copies:
        copy.wait()
    flat[...] = gram[...].reshape(k, k) / total

    def joined(j, c):
        return own[c * CP + KEPT : (c + 1) * CP] + once[j]

    for copy in first:
        copy.wait()
    second = [
        remote(once.at[2 * j + 1], twice.at[j], tree_send.at[4 + j], tree_recv.at[4 + j], behind(2))
        for j in range(W // 4)
    ]
    for j in range(W // 2):
        once[j] = joined(j, 2 * j)
    for copy in second:
        copy.start()
    third = remote(once.at[2], thrice, tree_send.at[6], tree_recv.at[6], behind(4))

    def between():
        for copy in second:
            copy.wait()
        once[2] = once[2] + twice[1]
        once[0] = once[0] + twice[0]
        third.start()

    factored(flat, r_ref, w_ref, work, cross, between)

    third.wait()
    once[0] = once[0] + thrice[...]
    last = pltpu.make_async_copy(once.at[0], got.at[pl.ds(W * KEPT, CP - KEPT)], keep_sem.at[1])
    last.start()
    for copy in straight:
        copy.wait()
    keep.wait()
    last.wait()


def moved_and_factored(held, total):
    bulk, wide = lax.axis_size("bulk"), lax.axis_size("wide")
    slots, blk, k = held.shape
    rest = CP - KEPT
    vmem, dma = pltpu.VMEM, pltpu.SemaphoreType.DMA
    return pl.pallas_call(
        functools.partial(window, bulk, wide, total),
        out_shape=[
            jax.ShapeDtypeStruct((W * KEPT + rest, blk, k), F32),
            jax.ShapeDtypeStruct((k, k), F32),
            jax.ShapeDtypeStruct((k, k), F32),
        ],
        in_specs=[pl.BlockSpec(memory_space=pltpu.HBM)],
        out_specs=[
            pl.BlockSpec(memory_space=pl.ANY),
            pl.BlockSpec(memory_space=vmem),
            pl.BlockSpec(memory_space=vmem),
        ],
        scratch_shapes=[
            vmem((slots, blk, k), F32),
            vmem((wide, k // wide, k), F32),
            vmem((wide, k // wide, k), F32),
            vmem((bulk, k // wide, k), F32),
            vmem((wide, k // wide, k), F32),
            vmem((k, k), F32),
            vmem((HALF, HALF), F32),
            vmem((HALF, HALF), F32),
            vmem((W // 2, rest, blk, k), F32),
            vmem((W // 4, rest, blk, k), F32),
            vmem((rest, blk, k), F32),
            dma((W,)), dma((wide,)), dma((wide,)), dma((bulk,)), dma((bulk,)), dma((wide,)), dma((wide,)),
            dma((W,)), dma((W,)), dma((W,)), dma((W,)), dma((2,)),
        ],
        compiler_params=pltpu.CompilerParams(
            collective_id=0, has_side_effects=True, vmem_limit_bytes=40 * 2**20
        ),
        name="window",
    )(held)


GROUP = 4


def solve_kernel(slot, got, w_ref, q_ref, w_high, w_low):
    step = pl.program_id(0)
    rest = CP - KEPT

    @pl.when(step == 0)
    def _():
        w_high[...], w_low[...] = split(w_ref[...])

    blocks = []
    for g in range(GROUP):
        s = slot[step * GROUP + g]
        c, i = s // CP, lax.rem(s, CP)
        blocks.append(got[jnp.where(i < KEPT, c * KEPT + i, W * KEPT + i - KEPT)])
    high, low = split(jnp.concatenate(blocks, axis=0))
    over = ((1,), (1,))
    q_ref[...] = (
        half_dot(low, w_high[...], over) + half_dot(high, w_low[...], over) + half_dot(high, w_high[...], over)
    )


def solved(got, w, source_slot):
    count, (_, blk, k) = source_slot.shape[0], got.shape
    return pl.pallas_call(
        solve_kernel,
        grid_spec=pltpu.PrefetchScalarGridSpec(
            num_scalar_prefetch=1,
            grid=(count // GROUP,),
            in_specs=[
                pl.BlockSpec(got.shape, lambda i, s: (0, 0, 0)),
                pl.BlockSpec((k, k), lambda i, s: (0, 0)),
            ],
            out_specs=pl.BlockSpec((GROUP * blk, k), lambda i, s: (i, 0)),
            scratch_shapes=[pltpu.VMEM((k, k), BF16), pltpu.VMEM((k, k), BF16)],
        ),
        out_shape=jax.ShapeDtypeStruct((count * blk, k), F32),
        compiler_params=pltpu.CompilerParams(vmem_limit_bytes=24 * 2**20),
        name="solve",
    )(source_slot, got, w)


def local(held, source_slot):
    total = lax.axis_size("bulk") * lax.axis_size("wide") * source_slot.shape[0] * held.shape[1]
    got, r_factor, w = moved_and_factored(held, total)
    return (solved(got, w, source_slot), r_factor)


def solution(mesh):
    in_specs = (P(("bulk", "wide"), None, None), P(("bulk", "wide")))
    out_specs = (P(("bulk", "wide"), None), P())
    return jax.shard_map(local, mesh=mesh, in_specs=in_specs, out_specs=out_specs, check_vma=False)
```

time: 249 us -> 134 us (0.54)
  the two profiles are of different devices: /device:TPU:24 before, /device:TPU:1 now
where the time goes in v1:
time: 134 us
  Pallas kernels  131 us (98%)
  local copies, waits for them, and re-layouts  2.89 us (2%)
    pallas_call x1, Pallas kernels, moved_and_factored(): pl.pallas_call(functools.partial(window, bulk, wide, total), out_shape=[j...  127 us
    pallas_call x1, Pallas kernels, solved(): pl.pallas_call(solve_kernel, grid_spec=pltpu.PrefetchScalarGridSpec(num_s...  3.43 us
    unnamed x5, local copies, waits for them, and re-layouts  2.89 us

profile of v1, /device:TPU:1, one launch (start us, length us, event | category | flops | bytes accessed | tf_op | source)
XLA Modules:
  0.0 134.1 jit_solution(6733478439847093586)
XLA Ops:
  0.6 0.0 copy-start
  0.6 2.2 %copy-done = f32[32,128,256]{2,1,0:T(8,128)S(1)} copy-done((f32[32,128,256]{2,1,0:T(8,128)S(1)}, f32[32,128,256]{2,1,0:T(8,128)}, u32[]{:S(2)}) %copy-start) | copy-done | bytes 4194328
  2.8 0.0 copy-start.1
  2.8 127.1 %window.1 = (f32[18,128,256]{2,1,0:T(8,128)S(1)}, f32[256,256]{1,0:T(8,128)S(1)}, f32[256,256]{1,0:T(8,128)S(1)}) custom-call(f32[32,128,256]{2,1,0:T(8,128)S(1)} %copy-done), custom_call_target="tpu_custom_call" | custom-call | tf_op jit(solution)/shard_map/window/pallas_call | solution.py:281
  129.9 0.0 copy-done.1
  129.9 3.4 %solve.1 = f32[2048,256]{1,0:T(8,128)} custom-call(s32[16]{0:T(128)S(1)} %copy-done.1, f32[18,128,256]{2,1,0:T(8,128)S(1)} %get-tuple-element.5.got, f32[256,256]{1,0:T(8,128)S(1)} %get-tuple-element.6.w_ref), custom_call_target="tpu_custom_call" | custom-call | tf_op jit(solution)/shard_map/solve/pallas_call | solution.py:341
  133.4 0.7 copy.5
Async XLA Ops:
  0.6 2.2 %copy-start = (f32[32,128,256]{2,1,0:T(8,128)S(1)}, f32[32,128,256]{2,1,0:T(8,128)}, u32[]{:S(2)}) copy-start(f32[32,128,256]{2,1,0:T(8,128)} %held.1) | copy-start | bytes 12582916
  2.8 127.1 %copy-start.1 = (s32[16]{0:T(128)S(1)}, s32[16]{0:T(128)}, u32[]{:S(2)}) copy-start(s32[16]{0:T(128)} %slot.1) | copy-start | bytes 196

commit v2 on v1

--- a/solution.py
+++ b/solution.py
@@ -10,6 +10,9 @@
 CP = 4
 W = 8
 KEPT = 2
+EARLY, LATE = (7, 6, 5, 4), (3, 2, 1)
+ROW_AT = 0
+VMEM = 40 * 2**20
 MESH = pl.DeviceIdType.MESH
 TILE = 8
 HALF = 128
@@ -137,13 +140,14 @@
 def window(
     bulk, wide, total,
     held, got, r_ref, w_ref,
-    own, acc, parts, shares, gram, flat, work, cross, once, twice, thrice,
+    own, acc, parts, shares, gram, flat, work, cross, across, sums, down,
     load_sem, part_send, part_recv, share_send, share_recv, gram_send, gram_recv,
-    slab_send, slab_recv, tree_send, tree_recv, keep_sem,
+    slab_send, slab_recv, row_send, row_recv, down_send, down_recv, keep_sem,
 ):
     my_bulk, my_wide = lax.axis_index("bulk"), lax.axis_index("wide")
     me = my_bulk * wide + my_wide
     devices = bulk * wide
+    column = lax.rem(my_wide, CP)
 
     def along_wide(o):
         return (my_bulk, lax.rem(my_wide + o, wide))
@@ -154,44 +158,28 @@
     def behind(c):
         to = lax.rem(me + devices - c, devices)
         return (to // wide, lax.rem(to, wide))
+
+    def in_row(b):
+        return (my_bulk, my_wide - column + lax.rem(column + CP - b, CP))
 
     def remote(src, dst, send, recv, to):
         return pltpu.make_async_remote_copy(
             src_ref=src, dst_ref=dst, send_sem=send, recv_sem=recv, device_id=to, device_id_type=MESH
         )
 
+    barrier = pltpu.get_barrier_semaphore()
+    peers = [along_wide(o) for o in range(1, wide)] + [along_bulk(o) for o in range(1, bulk)]
+    far = [*range(1, W), 2 * CP]
+    peers += [behind(c) for c in far] + [behind(devices - c) for c in far]
+    for peer in peers:
+        pl.semaphore_signal(barrier, inc=1, device_id=peer, device_id_type=MESH)
+
     loads = [
         pltpu.make_async_copy(held.at[pl.ds(c * CP, CP)], own.at[pl.ds(c * CP, CP)], load_sem.at[c])
         for c in range(W)
     ]
     for load in loads:
         load.start()
-
-    barrier = pltpu.get_barrier_semaphore()
-    peers = [along_wide(o) for o in range(1, wide)] + [along_bulk(o) for o in range(1, bulk)]
-    peers += [behind(c) for c in range(1, W)] + [behind(devices - c) for c in range(1, W)]
-    for peer in peers:
-        pl.semaphore_signal(barrier, inc=1, device_id=peer, device_id_type=MESH)
-    pl.semaphore_wait(barrier, len(peers))
-
-    first = [
-        remote(
-            held.at[pl.ds((2 * j + 1) * CP + KEPT, CP - KEPT)], once.at[j],
-            tree_send.at[j], tree_recv.at[j], behind(1),
-        )
-        for j in range(W // 2)
-    ]
-    for copy in first:
-        copy.start()
-    straight = [
-        remote(
-            held.at[pl.ds(c * CP, KEPT)], got.at[pl.ds(c * KEPT, KEPT)],
-            slab_send.at[c], slab_recv.at[c], behind(c),
-        )
-        for c in range(1, W)
-    ]
-    for copy in straight:
-        copy.start()
     keep = pltpu.make_async_copy(held.at[pl.ds(0, KEPT)], got.at[pl.ds(0, KEPT)], keep_sem.at[0])
     keep.start()
 
@@ -204,71 +192,97 @@
         mixed += half_dot(high, low, ((0,), (0,)))
     acc[...] = (square + mixed + mixed.T).reshape(acc.shape)
 
-    copies = [
+    pl.semaphore_wait(barrier, len(peers))
+
+    part_copies = [
         remote(acc.at[along_wide(o)[1]], parts.at[o], part_send.at[o], part_recv.at[o], along_wide(o))
         for o in range(1, wide)
     ]
-    for copy in copies:
+    for copy in part_copies:
         copy.start()
+
+    row_copies = [
+        remote(
+            held.at[pl.ds(c * CP + KEPT, CP - KEPT)], across.at[c],
+            row_send.at[c], row_recv.at[c], in_row(c % CP),
+        )
+        for c in range(W) if c % CP
+    ]
+    for copy in row_copies:
+        copy.start()
+    straight = {
+        c: remote(
+            held.at[pl.ds(c * CP, KEPT)], got.at[pl.ds(c * KEPT, KEPT)],
+            slab_send.at[c], slab_recv.at[c], behind(c),
+        )
+        for c in range(1, W)
+    }
+    for c in EARLY:
+        straight[c].start()
+
     share = acc[my_wide]
     for o in range(1, wide):
-        copies[o - 1].wait_recv()
+        part_copies[o - 1].wait_recv()
         share += parts[o]
     shares[my_bulk] = share
-    for copy in copies:
-        copy.wait_send()
-    copies = [
+    share_copies = [
         remote(shares.at[my_bulk], shares.at[my_bulk], share_send.at[o], share_recv.at[o], along_bulk(o))
         for o in range(1, bulk)
     ]
-    for copy in copies:
+    for copy in share_copies:
         copy.start()
-    for copy in copies:
+    for copy in part_copies:
+        copy.wait_send()
+    for copy in share_copies:
         copy.wait()
     share = shares[0]
     for b in range(1, bulk):
         share += shares[b]
     gram[my_wide] = share
-    copies = [
+    gram_copies = [
         remote(gram.at[my_wide], gram.at[my_wide], gram_send.at[o], gram_recv.at[o], along_wide(o))
         for o in range(1, wide)
     ]
-    for copy in copies:
+    for copy in gram_copies:
         copy.start()
-    for copy in copies:
+    for c in LATE:
+        straight[c].start()
+    for copy in gram_copies:
         copy.wait()
     flat[...] = gram[...].reshape(k, k) / total
 
-    def joined(j, c):
-        return own[c * CP + KEPT : (c + 1) * CP] + once[j]
-
-    for copy in first:
+    down_copies = [
+        remote(sums.at[i], down.at[i], down_send.at[i], down_recv.at[i], behind(CP * i)) for i in (1, 2)
+    ]
+
+    def next_row():
+        for copy in row_copies:
+            copy.wait()
+        mine = [own[KEPT:CP], own[CP * CP + KEPT : CP * CP + CP], jnp.zeros(sums.shape[1:], F32)]
+        for b in range(1, CP):
+            near, far = across[b], across[b + CP]
+            inside = column + b < CP
+            mine[0] += jnp.where(inside, near, 0.0)
+            mine[1] += jnp.where(inside, far, near)
+            mine[2] += jnp.where(inside, 0.0, far)
+        for i in range(3):
+            sums[i] = mine[i]
+        for copy in down_copies:
+            copy.start()
+
+    if ROW_AT == 0:
+        next_row()
+    factored(flat, r_ref, w_ref, work, cross, next_row if ROW_AT == 1 else lambda: None)
+    if ROW_AT == 2:
+        next_row()
+
+    for copy in down_copies:
         copy.wait()
-    second = [
-        remote(once.at[2 * j + 1], twice.at[j], tree_send.at[4 + j], tree_recv.at[4 + j], behind(2))
-        for j in range(W // 4)
-    ]
-    for j in range(W // 2):
-        once[j] = joined(j, 2 * j)
-    for copy in second:
-        copy.start()
-    third = remote(once.at[2], thrice, tree_send.at[6], tree_recv.at[6], behind(4))
-
-    def between():
-        for copy in second:
-            copy.wait()
-        once[2] = once[2] + twice[1]
-        once[0] = once[0] + twice[0]
-        third.start()
-
-    factored(flat, r_ref, w_ref, work, cross, between)
-
-    third.wait()
-    once[0] = once[0] + thrice[...]
-    last = pltpu.make_async_copy(once.at[0], got.at[pl.ds(W * KEPT, CP - KEPT)], keep_sem.at[1])
+    sums[0] = sums[0] + down[1] + down[2]
+    last = pltpu.make_async_copy(sums.at[0], got.at[pl.ds(W * KEPT, CP - KEPT)], keep_sem.at[1])
     last.start()
-    for copy in straight:
-        copy.wait()
+    for c in (*EARLY, *LATE):
+        straight[c].wait()
     keep.wait()
     last.wait()
 
@@ -300,14 +314,14 @@
             vmem((k, k), F32),
             vmem((HALF, HALF), F32),
             vmem((HALF, HALF), F32),
-            vmem((W // 2, rest, blk, k), F32),
-            vmem((W // 4, rest, blk, k), F32),
-            vmem((rest, blk, k), F32),
+            vmem((W, rest, blk, k), F32),
+            vmem((3, rest, blk, k), F32),
+            vmem((3, rest, blk, k), F32),
             dma((W,)), dma((wide,)), dma((wide,)), dma((bulk,)), dma((bulk,)), dma((wide,)), dma((wide,)),
-            dma((W,)), dma((W,)), dma((W,)), dma((W,)), dma((2,)),
+            dma((W,)), dma((W,)), dma((W,)), dma((W,)), dma((3,)), dma((3,)), dma((2,)),
         ],
         compiler_params=pltpu.CompilerParams(
-            collective_id=0, has_side_effects=True, vmem_limit_bytes=40 * 2**20
+            collective_id=0, has_side_effects=True, vmem_limit_bytes=VMEM
         ),
         name="window",
     )(held)

time: 134 us -> 81.5 us (0.61)
  the two profiles are of different devices: /device:TPU:1 before, /device:TPU:9 now
where the time goes in v2:
time: 81.5 us; the launch traced here: 79.9 us
  Pallas kernels  76.3 us (94%)
  local copies, waits for them, and re-layouts  2.89 us (4%)
    pallas_call x1, Pallas kernels, moved_and_factored(): pl.pallas_call(functools.partial(window, bulk, wide, total), out_shape=[j...  72.9 us
    pallas_call x1, Pallas kernels, solved(): pl.pallas_call(solve_kernel, grid_spec=pltpu.PrefetchScalarGridSpec(num_s...  3.42 us
    unnamed x5, local copies, waits for them, and re-layouts  2.89 us

profile of v2, /device:TPU:9, one launch (start us, length us, event | category | flops | bytes accessed | tf_op | source)
XLA Modules:
  0.0 79.9 jit_solution(2319062941413840087)
XLA Ops:
  0.6 0.0 copy-start
  0.6 2.2 %copy-done = f32[32,128,256]{2,1,0:T(8,128)S(1)} copy-done((f32[32,128,256]{2,1,0:T(8,128)S(1)}, f32[32,128,256]{2,1,0:T(8,128)}, u32[]{:S(2)}) %copy-start) | copy-done | bytes 4194328
  2.8 0.0 copy-start.1
  2.8 72.9 %window.1 = (f32[18,128,256]{2,1,0:T(8,128)S(1)}, f32[256,256]{1,0:T(8,128)S(1)}, f32[256,256]{1,0:T(8,128)S(1)}) custom-call(f32[32,128,256]{2,1,0:T(8,128)S(1)} %copy-done), custom_call_target="tpu_custom_call" | custom-call | tf_op jit(solution)/shard_map/window/pallas_call | solution.py:295
  75.7 0.0 copy-done.1
  75.8 3.4 %solve.1 = f32[2048,256]{1,0:T(8,128)} custom-call(s32[16]{0:T(128)S(1)} %copy-done.1, f32[18,128,256]{2,1,0:T(8,128)S(1)} %get-tuple-element.5.got, f32[256,256]{1,0:T(8,128)S(1)} %get-tuple-element.6.w_ref), custom_call_target="tpu_custom_call" | custom-call | tf_op jit(solution)/shard_map/solve/pallas_call | solution.py:355
  79.2 0.7 copy.5
Async XLA Ops:
  0.6 2.2 %copy-start = (f32[32,128,256]{2,1,0:T(8,128)S(1)}, f32[32,128,256]{2,1,0:T(8,128)}, u32[]{:S(2)}) copy-start(f32[32,128,256]{2,1,0:T(8,128)} %held.1) | copy-start | bytes 12582916
  2.8 72.9 %copy-start.1 = (s32[16]{0:T(128)S(1)}, s32[16]{0:T(128)}, u32[]{:S(2)}) copy-start(s32[16]{0:T(128)} %slot.1) | copy-start | bytes 196

commit v3 on v2

v3 whole, which is shorter than its diff:
```python
import functools

import jax
import jax.numpy as jnp
from jax import lax
from jax.experimental import pallas as pl
from jax.experimental.pallas import tpu as pltpu
from jax.sharding import PartitionSpec as P

CP = 4
W = 8
KEPT = 2
def both(kind, c):
    return ((kind, c, 0), (kind, c, 1))


def rows(i, *cs):
    return tuple(("row", c, i) for c in cs)


PLAN = (
    both("slab", 4) + rows(0, 1, 3),
    (),
    (),
    rows(0, 5, 7, 2, 6) + rows(1, 1, 3, 5, 7, 2, 6)
    + both("slab", 7) + both("slab", 6) + both("slab", 5) + both("slab", 3) + both("slab", 2) + both("slab", 1),
    (),
    (),
)
ROW_AT = (1, 2)
SOLVE = (7, 6, 5, 4, 3, 2, 1, 0)
VMEM = 40 * 2**20
MESH = pl.DeviceIdType.MESH
TILE = 8
HALF = 128
F32 = jnp.float32
BF16 = jnp.bfloat16


def row_of(x, r):
    return jnp.broadcast_to(x[r : r + 1, :], x.shape)


def col_of(x, c):
    return jnp.broadcast_to(x[:, c : c + 1], x.shape)


def reciprocal(x):
    y = pl.reciprocal(x, approx=True)
    return y * (2.0 - x * y)


def panels(a):
    count = HALF // TILE
    a = list(a)
    sub = lax.broadcasted_iota(jnp.int32, (TILE, HALF), 0)
    lane = lax.broadcasted_iota(jnp.int32, (TILE, HALF), 1)
    e = [jnp.where(lane == sub + TILE * t, 1.0, 0.0) for t in range(count)]
    upper, inverse = [], []
    for p in range(count):
        at = TILE * p
        cols = [col_of(a[p], at + q) for q in range(TILE)]
        d = {(i, j): row_of(cols[j], i) for i in range(TILE) for j in range(i, TILE)}
        y, z, l, inv = [], [], {}, []
        for r in range(TILE):
            yr, zr = row_of(a[p], r), row_of(e[p], r)
            for q in range(r):
                yr = yr - l[r, q] * y[q]
                zr = zr - l[r, q] * z[q]
            y.append(yr)
            z.append(zr)
            inv.append(reciprocal(d[r, r]))
            for i in range(r + 1, TILE):
                l[i, r] = d[r, i] * inv[r]
            for i in range(r + 1, TILE):
                for j in range(i, TILE):
                    d[i, j] = d[i, j] - l[i, r] * d[r, j]
        scale = lax.rsqrt(d[0, 0])
        rows_y, rows_z = y[0] * scale, z[0] * scale
        for r in range(1, TILE):
            scale = lax.rsqrt(d[r, r])
            rows_y = jnp.where(sub == r, y[r] * scale, rows_y)
            rows_z = jnp.where(sub == r, z[r] * scale, rows_z)
        upper.append(jnp.where(lane >= sub + at, rows_y, 0.0))
        inverse.append(jnp.where(lane <= sub + at, rows_z, 0.0))
        y = [y[r] * inv[r] for r in range(TILE)]
        z = [z[r] * inv[r] for r in range(TILE)]
        if p + 1 < count:
            c = [col_of(a[p + 1], at + q) for q in range(TILE)]
            for r in range(TILE):
                for q in range(r):
                    c[r] = c[r] - l[r, q] * c[q]
            for r in range(TILE):
                a[p + 1] = a[p + 1] - c[r] * y[r]
                e[p + 1] = e[p + 1] - c[r] * z[r]
        if p + 2 < count:
            for r in reversed(range(TILE)):
                for q in range(r + 1, TILE):
                    y[r] = y[r] - l[q, r] * y[q]
                    z[r] = z[r] - l[q, r] * z[q]
            for t in range(p + 2, count):
                c = [col_of(a[t], at + q) for q in range(TILE)]
                for r in range(TILE):
                    a[t] = a[t] - c[r] * y[r]
                    e[t] = e[t] - c[r] * z[r]
    return upper, inverse


def dot(x, y, over):
    return lax.dot_general(
        x, y, (over, ((), ())), precision=lax.Precision.HIGHEST, preferred_element_type=F32
    )


def split(x):
    high = x.astype(BF16)
    return high, (x - high.astype(F32)).astype(BF16)


def half_dot(x, y, over):
    return lax.dot_general(x, y, (over, ((), ())), preferred_element_type=F32)


def factored(gram, r_ref, w_ref, work, cross, between):
    n = HALF
    work[...] = gram[0:n, 0:n]
    r_ref[n:, 0:n] = jnp.zeros((n, n), F32)
    w_ref[0:n, n:] = jnp.zeros((n, n), F32)

    def half(h, carry):
        up, inv = panels([work[TILE * t : TILE * (t + 1), :] for t in range(n // TILE)])

        @pl.when(h == 0)
        def _():
            for t in range(n // TILE):
                r_ref[TILE * t : TILE * (t + 1), 0:n] = up[t]
                w_ref[TILE * t : TILE * (t + 1), 0:n] = inv[t]
            w = w_ref[0:n, 0:n]
            right = dot(w, gram[0:n, n:], ((1,), (0,)))
            r_ref[0:n, n:] = right
            work[...] = gram[n:, n:] - dot(right, right, ((0,), (0,)))
            cross[...] = dot(right, w, ((0,), (0,)))
            between()

        @pl.when(h == 1)
        def _():
            for t in range(n // TILE):
                r_ref[n + TILE * t : n + TILE * (t + 1), n:] = up[t]
                w_ref[n + TILE * t : n + TILE * (t + 1), n:] = inv[t]
            w_ref[n:, 0:n] = -dot(w_ref[n:, n:], cross[...], ((1,), (0,)))

        return carry

    lax.fori_loop(0, 2, half, 0)


def window(
    bulk, wide, total,
    slots, held, q_ref, r_ref,
    slot, slot_sem,     w_ref, solved, own, land, acc, parts, shares, columns, chunk, gram, flat, work, cross, across, sums, down, w_high, w_low,
    load_sem, part_send, part_recv, share_send, share_recv, column_send, column_recv, piece_send, piece_recv,
    gram_send, gram_recv, slab_send, slab_recv, row_send, row_recv, down_send, down_recv,
):
    my_bulk, my_wide = lax.axis_index("bulk"), lax.axis_index("wide")
    me = my_bulk * wide + my_wide
    devices = bulk * wide
    column, row = lax.rem(my_wide, CP), my_wide // CP
    height = wide // CP

    def along_bulk(o):
        return (lax.rem(my_bulk + o, bulk), my_wide)

    def behind(c):
        to = lax.rem(me + devices - c, devices)
        return (to // wide, lax.rem(to, wide))

    def in_row(b):
        return (my_bulk, row * CP + lax.rem(column + CP - b, CP))

    def in_column(b):
        return (my_bulk, lax.rem(row + height - b, height) * CP + column)

    def remote(src, dst, send, recv, to):
        return pltpu.make_async_remote_copy(
            src_ref=src, dst_ref=dst, send_sem=send, recv_sem=recv, device_id=to, device_id_type=MESH
        )

    barrier = pltpu.get_barrier_semaphore()
    far = [*range(1, W), 2 * CP]
    peers = [behind(c) for c in far] + [behind(devices - c) for c in far]
    peers += [in_column(b) for b in range(1, height)] + [along_bulk(o) for o in range(1, bulk)]
    for peer in peers:
        pl.semaphore_signal(barrier, inc=1, device_id=peer, device_id_type=MESH)

    loads = [
        pltpu.make_async_copy(held.at[pl.ds(c * CP, CP)], own.at[pl.ds(c * CP, CP)], load_sem.at[c])
        for c in range(W)
    ]
    for load in loads:
        load.start()
    places = pltpu.make_async_copy(slots, slot, slot_sem.at[0])
    places.start()

    rows, k = CP * own.shape[1], own.shape[2]
    square, mixed = jnp.zeros((k, k), F32), jnp.zeros((k, k), F32)
    for c in range(W):
        loads[c].wait()
        high, low = split(own[c * CP : (c + 1) * CP].reshape(rows, k))
        square += half_dot(high, high, ((0,), (0,))) + half_dot(low, low, ((0,), (0,)))
        mixed += half_dot(high, low, ((0,), (0,)))
    acc[...] = (square + mixed + mixed.T).reshape(acc.shape)

    pl.semaphore_wait(barrier, len(peers))

    part_copies = [
        remote(acc.at[along_bulk(o)[0]], parts.at[o], part_send.at[o], part_recv.at[o], along_bulk(o))
        for o in range(1, bulk)
    ]
    for copy in part_copies:
        copy.start()

    large = {}
    for c in range(1, W):
        for i in range(KEPT):
            large["slab", c, i] = remote(
                held.at[c * CP + i], land.at[c * KEPT + i], slab_send.at[c, i], slab_recv.at[c, i], behind(c)
            )
            if c % CP:
                large["row", c, i] = remote(
                    held.at[c * CP + KEPT + i], across.at[c, i],
                    row_send.at[c, i], row_recv.at[c, i], in_row(c % CP),
                )

    def begin(point):
        for key in PLAN[point]:
            large[key].start()

    begin(0)

    part = acc[my_bulk]
    for o in range(1, bulk):
        part_copies[o - 1].wait_recv()
        part += parts[o]
    shares[0] = part.reshape(shares.shape[1:])
    share_copies = [
        remote(shares.at[0, lax.rem(column + CP - b, CP)], shares.at[b, 0], share_send.at[b], share_recv.at[b], in_row(b))
        for b in range(1, CP)
    ]
    for copy in share_copies:
        copy.start()
    begin(1)
    for copy in part_copies:
        copy.wait_send()
    share = shares[0, column]
    for b in range(1, CP):
        share_copies[b - 1].wait_recv()
        share += shares[b, 0]
    columns[row] = share
    column_copies = [
        remote(columns.at[row], columns.at[row], column_send.at[b], column_recv.at[b], in_column(b))
        for b in range(1, height)
    ]
    for copy in column_copies:
        copy.start()
    begin(2)
    for copy in share_copies:
        copy.wait_send()
    for copy in column_copies:
        copy.wait()
    share = columns[0]
    for b in range(1, height):
        share += columns[b]
    chunk[column] = share
    piece_copies = [
        remote(chunk.at[column], chunk.at[column], piece_send.at[b], piece_recv.at[b], in_row(b))
        for b in range(1, CP)
    ]
    for copy in piece_copies:
        copy.start()
    begin(3)
    for copy in piece_copies:
        copy.wait()
    gram[my_bulk] = chunk[...].reshape(gram.shape[1:])
    gram_copies = [
        remote(gram.at[my_bulk], gram.at[my_bulk], gram_send.at[o], gram_recv.at[o], along_bulk(o))
        for o in range(1, bulk)
    ]
    for copy in gram_copies:
        copy.start()
    begin(4)
    for copy in gram_copies:
        copy.wait()
    flat[...] = gram[...].reshape(k, k) / total

    begin(5)

    down_copies = [
        [
            remote(sums.at[i, n], down.at[i, n], down_send.at[i, n], down_recv.at[i, n], behind(CP * i))
            for i in (1, 2)
        ]
        for n in range(CP - KEPT)
    ]

    def next_row(n):
        for key, copy in large.items():
            if key[0] == "row" and key[2] == n:
                copy.wait()
        mine = [own[KEPT + n], own[CP * CP + KEPT + n], jnp.zeros(sums.shape[2:], F32)]
        for b in range(1, CP):
            near, far = across[b, n], across[b + CP, n]
            inside = column + b < CP
            mine[0] += jnp.where(inside, near, 0.0)
            mine[1] += jnp.where(inside, far, near)
            mine[2] += jnp.where(inside, 0.0, far)
        for i in range(3):
            sums[i, n] = mine[i]
        for copy in down_copies[n]:
            copy.start()

    def at_point(point):
        for n in range(CP - KEPT):
            if ROW_AT[n] == point:
                next_row(n)

    at_point(0)
    factored(flat, r_ref, w_ref, work, cross, functools.partial(at_point, 1))
    at_point(2)
    w_high[...], w_low[...] = split(w_ref[...])

    def solve(blocks, at):
        high, low = split(blocks.reshape(-1, k))
        over = ((1,), (1,))
        q = half_dot(low, w_high[...], over) + half_dot(high, w_low[...], over) + half_dot(high, w_high[...], over)
        solved[at : at + blocks.shape[0]] = q.reshape(blocks.shape)

    solve(own[0:KEPT], 0)
    for c in SOLVE:
        if c:
            for i in range(KEPT):
                large["slab", c, i].wait()
            solve(land[c * KEPT : (c + 1) * KEPT], c * KEPT)
        else:
            for n in range(CP - KEPT):
                for copy in down_copies[n]:
                    copy.wait()
            solve(sums[0] + down[1] + down[2], W * KEPT)

    places.wait()
    blk = own.shape[1]
    for j in range(q_ref.shape[0] // blk):
        c, i = slot[j] // CP, lax.rem(slot[j], CP)
        q_ref[j * blk : (j + 1) * blk] = solved[jnp.where(i < KEPT, c * KEPT + i, W * KEPT + i - KEPT)]


def moved_and_solved(held, source_slot, total):
    bulk, wide = lax.axis_size("bulk"), lax.axis_size("wide")
    slots, blk, k = held.shape
    rest = CP - KEPT
    vmem, dma = pltpu.VMEM, pltpu.SemaphoreType.DMA
    return pl.pallas_call(
        functools.partial(window, bulk, wide, total),
        out_shape=[
            jax.ShapeDtypeStruct((source_slot.shape[0] * blk, k), F32),
            jax.ShapeDtypeStruct((k, k), F32),
        ],
        in_specs=[pl.BlockSpec(memory_space=pl.ANY)] * 2,
        out_specs=[pl.BlockSpec(memory_space=vmem)] * 2,
        scratch_shapes=[
            pltpu.SMEM(source_slot.shape, jnp.int32),
            dma((1,)),
            vmem((k, k), F32),
            vmem((W * KEPT + rest, blk, k), F32),
            vmem((slots, blk, k), F32),
            vmem((W * KEPT, blk, k), F32),
            vmem((bulk, k // bulk, k), F32),
            vmem((bulk, k // bulk, k), F32),
            vmem((CP, CP, k // bulk // CP, k), F32),
            vmem((wide // CP, k // bulk // CP, k), F32),
            vmem((CP, k // bulk // CP, k), F32),
            vmem((bulk, k // bulk, k), F32),
            vmem((k, k), F32),
            vmem((HALF, HALF), F32),
            vmem((HALF, HALF), F32),
            vmem((W, rest, blk, k), F32),
            vmem((3, rest, blk, k), F32),
            vmem((3, rest, blk, k), F32),
            vmem((k, k), BF16),
            vmem((k, k), BF16),
            dma((W,)), dma((bulk,)), dma((bulk,)), dma((CP,)), dma((CP,)), dma((wide // CP,)), dma((wide // CP,)),
            dma((CP,)), dma((CP,)), dma((bulk,)), dma((bulk,)),
            dma((W, KEPT)), dma((W, KEPT)), dma((W, KEPT)), dma((W, KEPT)), dma((3, rest)), dma((3, rest)),
        ],
        compiler_params=pltpu.CompilerParams(
            collective_id=0, has_side_effects=True, vmem_limit_bytes=VMEM
        ),
        name="window",
    )(source_slot, held)


def local(held, source_slot):
    total = lax.axis_size("bulk") * lax.axis_size("wide") * source_slot.shape[0] * held.shape[1]
    return tuple(moved_and_solved(held, source_slot, total))


def solution(mesh):
    in_specs = (P(("bulk", "wide"), None, None), P(("bulk", "wide")))
    out_specs = (P(("bulk", "wide"), None), P())
    return jax.shard_map(local, mesh=mesh, in_specs=in_specs, out_specs=out_specs, check_vma=False)
```

time: 81.5 us -> 77.4 us (0.950)
  the two profiles are of different devices: /device:TPU:9 before, /device:TPU:88 now
where the time goes in v3:
time: 77.4 us; the launch traced here: 77.2 us
  Pallas kernels  71.7 us (93%)
  local copies, waits for them, and re-layouts  4.86 us (6%)
    pallas_call x1, Pallas kernels, moved_and_solved(): pl.pallas_call(functools.partial(window, bulk, wide, total), out_shape=[j...  71.7 us
    unnamed x6, local copies, waits for them, and re-layouts  4.86 us

profile of v3, /device:TPU:88, one launch (start us, length us, event | category | flops | bytes accessed | tf_op | source)
XLA Modules:
  0.0 77.2 jit_solution(10212629375232284655)
XLA Ops:
  0.6 0.0 copy-start
  0.6 2.2 %copy-done = f32[32,128,256]{2,1,0:T(8,128)S(1)} copy-done((f32[32,128,256]{2,1,0:T(8,128)S(1)}, f32[32,128,256]{2,1,0:T(8,128)}, u32[]{:S(2)}) %copy-start) | copy-done | bytes 4194328
  2.8 0.0 copy-start.1
  2.8 0.7 copy-done.1
  3.5 71.7 %window.1 = (f32[2048,256]{1,0:T(8,128)S(1)}, f32[256,256]{1,0:T(8,128)S(1)}) custom-call(s32[16]{0:T(128)S(1)} %copy-done.1, f32[32,128,256]{2,1,0:T(8,128)S(1)} %copy-done), custom_call_target="tpu_custom_call" | custom-call | tf_op jit(solution)/shard_map/window/pallas_call | solution.py:361
  75.2 1.3 %copy.6 = f32[2048,256]{1,0:T(8,128)} copy(f32[2048,256]{1,0:T(8,128)S(1)} %get-tuple-element.4) | data formatting | bytes 4194304
  76.5 0.7 copy.7
Async XLA Ops:
  0.6 2.2 %copy-start = (f32[32,128,256]{2,1,0:T(8,128)S(1)}, f32[32,128,256]{2,1,0:T(8,128)}, u32[]{:S(2)}) copy-start(f32[32,128,256]{2,1,0:T(8,128)} %held.1) | copy-start | bytes 12582916
  2.8 0.7 copy-start.1

commit v4 on v3

--- a/solution.py
+++ b/solution.py
@@ -20,16 +20,16 @@
 
 PLAN = (
     both("slab", 4) + rows(0, 1, 3),
-    (),
-    (),
-    rows(0, 5, 7, 2, 6) + rows(1, 1, 3, 5, 7, 2, 6)
-    + both("slab", 7) + both("slab", 6) + both("slab", 5) + both("slab", 3) + both("slab", 2) + both("slab", 1),
+    rows(0, 5, 7),
+    (("slab", 7, 0),),
+    rows(0, 2, 6) + rows(1, 1, 3) + (("slab", 7, 1),) + rows(1, 5, 7) + both("slab", 6) + rows(1, 2, 6)
+    + both("slab", 5) + both("slab", 3) + both("slab", 1) + both("slab", 2),
     (),
     (),
 )
 ROW_AT = (1, 2)
 SOLVE = (7, 6, 5, 4, 3, 2, 1, 0)
-VMEM = 40 * 2**20
+VMEM = 50 * 2**20
 MESH = pl.DeviceIdType.MESH
 TILE = 8
 HALF = 128

time: 77.4 us -> 74.2 us (0.959)
  the two profiles are of different devices: /device:TPU:88 before, /device:TPU:9 now
where the time goes in v4:
time: 74.2 us; the launch traced here: 74.1 us
  Pallas kernels  70.8 us (95%)
  local copies, waits for them, and re-layouts  2.67 us (4%)
    pallas_call x1, Pallas kernels, moved_and_solved(): pl.pallas_call(functools.partial(window, bulk, wide, total), out_shape=[j...  70.8 us
    unnamed x4, local copies, waits for them, and re-layouts  2.67 us

profile of v4, /device:TPU:9, one launch (start us, length us, event | category | flops | bytes accessed | tf_op | source)
XLA Modules:
  0.0 74.1 jit_solution(15325701404171667687)
XLA Ops:
  0.6 0.0 copy-start
  0.6 0.6 copy-done
  1.3 70.8 %window.1 = (f32[2048,256]{1,0:T(8,128)S(1)}, f32[256,256]{1,0:T(8,128)S(1)}) custom-call(s32[16]{0:T(128)S(1)} %copy-done, f32[32,128,256]{2,1,0:T(8,128)} %held.1), custom_call_target="tpu_custom_call" | custom-call | tf_op jit(solution)/shard_map/window/pallas_call | solution.py:361
  72.1 1.3 %copy.6 = f32[2048,256]{1,0:T(8,128)} copy(f32[2048,256]{1,0:T(8,128)S(1)} %get-tuple-element.4) | data formatting | bytes 4194304
  73.4 0.7 copy.7
Async XLA Ops:
  0.6 0.7 copy-start

commit v5 on v4

--- a/solution.py
+++ b/solution.py
@@ -10,8 +10,8 @@
 CP = 4
 W = 8
 KEPT = 2
-def both(kind, c):
-    return ((kind, c, 0), (kind, c, 1))
+def slabs(*cs):
+    return tuple(("slab", c, 0) for c in cs)
 
 
 def rows(i, *cs):
@@ -19,11 +19,10 @@
 
 
 PLAN = (
-    both("slab", 4) + rows(0, 1, 3),
+    slabs(4) + rows(0, 1, 3),
     rows(0, 5, 7),
-    (("slab", 7, 0),),
-    rows(0, 2, 6) + rows(1, 1, 3) + (("slab", 7, 1),) + rows(1, 5, 7) + both("slab", 6) + rows(1, 2, 6)
-    + both("slab", 5) + both("slab", 3) + both("slab", 1) + both("slab", 2),
+    slabs(7),
+    rows(0, 2, 6) + rows(1, 1, 3, 5, 7) + slabs(6) + rows(1, 2, 6) + slabs(5, 3, 1, 2),
     (),
     (),
 )
@@ -187,7 +186,7 @@
 
     barrier = pltpu.get_barrier_semaphore()
     far = [*range(1, W), 2 * CP]
-    peers = [behind(c) for c in far] + [behind(devices - c) for c in far]
+    peers = [behind(devices - c) for c in far] + [in_row(b) for b in range(1, CP)]
     peers += [in_column(b) for b in range(1, height)] + [along_bulk(o) for o in range(1, bulk)]
     for peer in peers:
         pl.semaphore_signal(barrier, inc=1, device_id=peer, device_id_type=MESH)
@@ -221,11 +220,11 @@
 
     large = {}
     for c in range(1, W):
-        for i in range(KEPT):
-            large["slab", c, i] = remote(
-                held.at[c * CP + i], land.at[c * KEPT + i], slab_send.at[c, i], slab_recv.at[c, i], behind(c)
-            )
-            if c % CP:
+        large["slab", c, 0] = remote(
+            held.at[pl.ds(c * CP, KEPT)], land.at[pl.ds(c * KEPT, KEPT)], slab_send.at[c], slab_recv.at[c], behind(c)
+        )
+        if c % CP:
+            for i in range(CP - KEPT):
                 large["row", c, i] = remote(
                     held.at[c * CP + KEPT + i], across.at[c, i],
                     row_send.at[c, i], row_recv.at[c, i], in_row(c % CP),
@@ -337,8 +336,7 @@
     solve(own[0:KEPT], 0)
     for c in SOLVE:
         if c:
-            for i in range(KEPT):
-                large["slab", c, i].wait()
+            large["slab", c, 0].wait()
             solve(land[c * KEPT : (c + 1) * KEPT], c * KEPT)
         else:
             for n in range(CP - KEPT):
@@ -389,7 +387,7 @@
             vmem((k, k), BF16),
             dma((W,)), dma((bulk,)), dma((bulk,)), dma((CP,)), dma((CP,)), dma((wide // CP,)), dma((wide // CP,)),
             dma((CP,)), dma((CP,)), dma((bulk,)), dma((bulk,)),
-            dma((W, KEPT)), dma((W, KEPT)), dma((W, KEPT)), dma((W, KEPT)), dma((3, rest)), dma((3, rest)),
+            dma((W,)), dma((W,)), dma((W, rest)), dma((W, rest)), dma((3, rest)), dma((3, rest)),
         ],
         compiler_params=pltpu.CompilerParams(
             collective_id=0, has_side_effects=True, vmem_limit_bytes=VMEM

time: 74.2 us -> 74 us (level)
  no operation moved by 1% of the time
where the time goes in v5:
time: 74 us; the launch traced here: 73.9 us
  Pallas kernels  70.6 us (95%)
  local copies, waits for them, and re-layouts  2.67 us (4%)
    pallas_call x1, Pallas kernels, moved_and_solved(): pl.pallas_call(functools.partial(window, bulk, wide, total), out_shape=[j...  70.6 us
    unnamed x4, local copies, waits for them, and re-layouts  2.67 us

profile of v5, /device:TPU:9, one launch (start us, length us, event | category | flops | bytes accessed | tf_op | source)
XLA Modules:
  0.0 73.9 jit_solution(15379433569151093415)
XLA Ops:
  0.6 0.0 copy-start
  0.6 0.6 copy-done
  1.3 70.6 %window.1 = (f32[2048,256]{1,0:T(8,128)S(1)}, f32[256,256]{1,0:T(8,128)S(1)}) custom-call(s32[16]{0:T(128)S(1)} %copy-done, f32[32,128,256]{2,1,0:T(8,128)} %held.1), custom_call_target="tpu_custom_call" | custom-call | tf_op jit(solution)/shard_map/window/pallas_call | solution.py:359
  71.9 1.3 %copy.6 = f32[2048,256]{1,0:T(8,128)} copy(f32[2048,256]{1,0:T(8,128)S(1)} %get-tuple-element.4) | data formatting | bytes 4194304
  73.2 0.7 copy.7
Async XLA Ops:
  0.6 0.7 copy-start

commit v6 on v5

--- a/solution.py
+++ b/solution.py
@@ -20,9 +20,9 @@
 
 PLAN = (
     slabs(4) + rows(0, 1, 3),
-    rows(0, 5, 7),
+    (),
     slabs(7),
-    rows(0, 2, 6) + rows(1, 1, 3, 5, 7) + slabs(6) + rows(1, 2, 6) + slabs(5, 3, 1, 2),
+    rows(0, 2) + rows(1, 1, 3, 2) + slabs(6, 5, 3, 2, 1),
     (),
     (),
 )
@@ -192,7 +192,7 @@
         pl.semaphore_signal(barrier, inc=1, device_id=peer, device_id_type=MESH)
 
     loads = [
-        pltpu.make_async_copy(held.at[pl.ds(c * CP, CP)], own.at[pl.ds(c * CP, CP)], load_sem.at[c])
+        pltpu.make_async_copy(held.at[c // CP, c % CP], own.at[pl.ds(c * CP, CP)], load_sem.at[c])
         for c in range(W)
     ]
     for load in loads:
@@ -221,13 +221,12 @@
     large = {}
     for c in range(1, W):
         large["slab", c, 0] = remote(
-            held.at[pl.ds(c * CP, KEPT)], land.at[pl.ds(c * KEPT, KEPT)], slab_send.at[c], slab_recv.at[c], behind(c)
+            held.at[c // CP, c % CP, pl.ds(0, KEPT)], land.at[pl.ds(c * KEPT, KEPT)], slab_send.at[c], slab_recv.at[c], behind(c)
         )
-        if c % CP:
+        if c < CP:
             for i in range(CP - KEPT):
                 large["row", c, i] = remote(
-                    held.at[c * CP + KEPT + i], across.at[c, i],
-                    row_send.at[c, i], row_recv.at[c, i], in_row(c % CP),
+                    held.at[:, c, KEPT + i], across.at[c, i], row_send.at[c, i], row_recv.at[c, i], in_row(c)
                 )
 
     def begin(point):
@@ -307,7 +306,7 @@
                 copy.wait()
         mine = [own[KEPT + n], own[CP * CP + KEPT + n], jnp.zeros(sums.shape[2:], F32)]
         for b in range(1, CP):
-            near, far = across[b, n], across[b + CP, n]
+            near, far = across[b, n, 0], across[b, n, 1]
             inside = column + b < CP
             mine[0] += jnp.where(inside, near, 0.0)
             mine[1] += jnp.where(inside, far, near)
@@ -380,20 +379,20 @@
             vmem((k, k), F32),
             vmem((HALF, HALF), F32),
             vmem((HALF, HALF), F32),
-            vmem((W, rest, blk, k), F32),
+            vmem((CP, rest, W // CP, blk, k), F32),
             vmem((3, rest, blk, k), F32),
             vmem((3, rest, blk, k), F32),
             vmem((k, k), BF16),
             vmem((k, k), BF16),
             dma((W,)), dma((bulk,)), dma((bulk,)), dma((CP,)), dma((CP,)), dma((wide // CP,)), dma((wide // CP,)),
             dma((CP,)), dma((CP,)), dma((bulk,)), dma((bulk,)),
-            dma((W,)), dma((W,)), dma((W, rest)), dma((W, rest)), dma((3, rest)), dma((3, rest)),
+            dma((W,)), dma((W,)), dma((CP, rest)), dma((CP, rest)), dma((3, rest)), dma((3, rest)),
         ],
         compiler_params=pltpu.CompilerParams(
             collective_id=0, has_side_effects=True, vmem_limit_bytes=VMEM
         ),
         name="window",
-    )(source_slot, held)
+    )(source_slot, held.reshape(W // CP, CP, CP, blk, k))
 
 
 def local(held, source_slot):

time: 74 us -> 73.3 us (level)
  no operation moved by 1% of the time
where the time goes in v6:
time: 73.3 us; the launch traced here: 73.2 us
  Pallas kernels  69.9 us (95%)
  local copies, waits for them, and re-layouts  2.67 us (4%)
    pallas_call x1, Pallas kernels, moved_and_solved(): pl.pallas_call(functools.partial(window, bulk, wide, total), out_shape=[j...  69.9 us
    unnamed x4, local copies, waits for them, and re-layouts  2.67 us

profile of v6, /device:TPU:9, one launch (start us, length us, event | category | flops | bytes accessed | tf_op | source)
XLA Modules:
  0.0 73.2 jit_solution(15637128973027388589)
XLA Ops:
  0.6 0.0 copy-start
  0.6 0.6 copy-done
  1.3 69.9 %window.1 = (f32[2048,256]{1,0:T(8,128)S(1)}, f32[256,256]{1,0:T(8,128)S(1)}) custom-call(s32[16]{0:T(128)S(1)} %copy-done, f32[2,4,4,128,256]{4,3,2,1,0:T(8,128)} %bitcast.1), custom_call_target="tpu_custom_call" | custom-call | tf_op jit(solution)/shard_map/window/pallas_call | solution.py:358
  71.2 1.3 %copy.6 = f32[2048,256]{1,0:T(8,128)} copy(f32[2048,256]{1,0:T(8,128)S(1)} %get-tuple-element.4) | data formatting | bytes 4194304
  72.5 0.7 copy.7
Async XLA Ops:
  0.6 0.7 copy-start
